TPU v7x, 512 devices: a whole 4x4x16 slice. The times are simulated.
512 devices in a mesh: ctx: 64 (over y, z), head: 8 (over x, core).
Axes of the slice: x: 4, y: 4, z: 16, core: 2. Of those that a mesh axis runs over, the one named last changes fastest.
Arguments:
- queries: bfloat16 [8192, 64, 576], P('ctx', 'head'), may hold values from -14 to 14
- latents: bfloat16 [8192, 576], P('ctx'), may hold values from -6 to 6
- grad_out: bfloat16 [8192, 64, 512], P('ctx', 'head'), may hold values from -6 to 6
- doc_ids: int32 [8192], replicated, may hold values from 0 to 8191, as said below
Outputs:
- grad_queries: bfloat16 [8192, 64, 576], P('ctx', 'head')
- grad_latents: bfloat16 [8192, 576], P('ctx')
Inputs may be any that keep to these rules, and one draw needn't show every extreme that they name: `doc_ids`: each document is a contiguous run of at most 1024 tokens, one has exactly that many, and its label is the position of its first token.
All inputs are finite; a program needn't handle non-finite values.
Results may differ from a plain program's by a relative error of at most 0.0052.
Values may be sent and summed in bfloat16 or wider, within the bound.
A program may use at most 64 MiB of HBM per device.

v0:
```python
import jax
import jax.numpy as jnp
from jax import lax
from jax.sharding import PartitionSpec as P

LAT_C = 512
ROPE = 64
SPAN = 8


score_scale = 192.0 ** (-0.5)


def passed_along(value, axis, steps):
    count = lax.axis_size(axis)
    leading, last = (max(0, -steps), min(count, count - steps))
    return lax.ppermute(value, axis, [(source, source + steps) for source in range(leading, last)])


def attend_backward(query_rows, grad_rows, key_rows, visible):
    value_rows = key_rows[:, :LAT_C]
    scores = (
        jnp.einsum("thc,kc->htk", query_rows, key_rows, preferred_element_type=jnp.float32)
        * score_scale
    )
    scores = jnp.where(visible[None], scores, -1e30)
    row_max = jnp.max(scores, axis=-1, keepdims=True)
    expo = jnp.where(visible[None], jnp.exp(scores - row_max), 0.0)
    weights = expo / jnp.sum(expo, axis=-1, keepdims=True)
    probs = weights.astype(jnp.bfloat16)
    output = jnp.einsum("htk,kc->thc", probs, value_rows, preferred_element_type=jnp.float32)
    delta = jnp.sum(grad_rows.astype(jnp.float32) * output, axis=-1)
    grad_probs = jnp.einsum(
        "thc,kc->htk", grad_rows, value_rows, preferred_element_type=jnp.float32
    )
    grad_scores = (weights * (grad_probs - jnp.transpose(delta)[:, :, None]) * score_scale).astype(
        jnp.bfloat16
    )
    grad_query = jnp.einsum(
        "htk,kc->thc", grad_scores, key_rows, preferred_element_type=jnp.float32
    ).astype(jnp.bfloat16)
    grad_keys = jnp.einsum(
        "htk,thc->kc", grad_scores, query_rows, preferred_element_type=jnp.float32
    )
    grad_values = jnp.einsum("htk,thc->kc", probs, grad_rows, preferred_element_type=jnp.float32)
    grad_keys = grad_keys + jnp.pad(grad_values, ((0, 0), (0, ROPE)))
    return (grad_query, grad_keys)


def return_owned(window_grads, tok_rows):
    owned = window_grads[SPAN * tok_rows :]
    for offset in range(1, SPAN + 1):
        piece = window_grads[(SPAN - offset) * tok_rows : (SPAN - offset + 1) * tok_rows]
        owned = owned + passed_along(piece, "ctx", -offset)
    return owned


def on_device(queries, latents, grad_out, doc_ids):
    tok_rows = latents.shape[0]
    window = (SPAN + 1) * tok_rows
    shard_index = lax.axis_index("ctx")
    pieces = []
    for offset in range(SPAN, 0, -1):
        pieces.append(passed_along(latents, "ctx", offset))
    pieces.append(latents)
    key_rows = jnp.concatenate(pieces, axis=0)
    start = shard_index * tok_rows
    padded_ids = jnp.concatenate([jnp.full((SPAN * tok_rows,), -1, jnp.int32), doc_ids], axis=0)
    key_ids = lax.dynamic_slice_in_dim(padded_ids, start, window, 0)
    query_ids = lax.dynamic_slice_in_dim(doc_ids, start, tok_rows, 0)
    query_pos = start + jnp.arange(tok_rows, dtype=jnp.int32)
    key_pos = start - SPAN * tok_rows + jnp.arange(window, dtype=jnp.int32)
    visible = (key_ids[None, :] == query_ids[:, None]) & (key_pos[None, :] <= query_pos[:, None])
    grad_query, grad_keys = attend_backward(queries, grad_out, key_rows, visible)
    owned = lax.psum(return_owned(grad_keys, tok_rows), "head")
    return (grad_query, owned.astype(jnp.bfloat16))


def solution(mesh):
    placed = (P("ctx", "head", None), P("ctx", None), P("ctx", "head", None), P())
    return jax.shard_map(
        on_device,
        mesh=mesh,
        in_specs=placed,
        out_specs=(P("ctx", "head", None), P("ctx", None)),
        check_vma=False,
    )
```

profile of v0, /device:TPU:16, one launch (start us, length us, event | category | flops | bytes accessed | tf_op | source)
XLA Modules:
  0.0 377.0 jit_solution(13197455609883375270)
XLA Ops:
  0.7 15.9 %collective-permute-start = (bf16[128,576]{0,1:T(8,128)(2,1)}, bf16[128,576]{0,1:T(8,128)(2,1)S(1)}, u32[]{:S(2)}, u32[]{:S(2)}) collective-permute-start(bf16[128,576]{0,1:T(8,128)(2,1)} %param.5), channel_id=1, source_target_pairs={{0,64},{8,72},{16,80},{24,88},{32,96},{40,104},{48,112},{56,120},{... | collective-permute-start | bytes 442376 | tf_op jit(solution)/shard_map/ppermute | solution.py:17
  16.5 5.7 %collective-permute-start.1 = (bf16[128,576]{0,1:T(8,128)(2,1)}, bf16[128,576]{0,1:T(8,128)(2,1)S(1)}, u32[]{:S(2)}, u32[]{:S(2)}) collective-permute-start(bf16[128,576]{0,1:T(8,128)(2,1)} %param.5), channel_id=1, source_target_pairs={{0,56},{8,64},{16,72},{24,80},{32,88},{40,96},{48,104},{56,112},{6... | collective-permute-start | bytes 442376 | tf_op jit(solution)/shard_map/ppermute | solution.py:17
  26.5 8.7 %collective-permute-start.3 = (bf16[128,576]{0,1:T(8,128)(2,1)}, bf16[128,576]{0,1:T(8,128)(2,1)S(1)}, u32[]{:S(2)}, u32[]{:S(2)}) collective-permute-start(bf16[128,576]{0,1:T(8,128)(2,1)} %param.5), channel_id=1, source_target_pairs={{0,40},{8,48},{16,56},{24,64},{32,72},{40,80},{48,88},{56,96},{64,... | collective-permute-start | bytes 442376 | tf_op jit(solution)/shard_map/ppermute | solution.py:17
  46.4 18.1 %collective-permute-done.1 = bf16[128,576]{0,1:T(8,128)(2,1)S(1)} collective-permute-done((bf16[128,576]{0,1:T(8,128)(2,1)}, bf16[128,576]{0,1:T(8,128)(2,1)S(1)}, u32[]{:S(2)}, u32[]{:S(2)}) %collective-permute-start.1) | collective-permute-done | bytes 147488 | tf_op jit(solution)/shard_map/ppermute | solution.py:17
  64.6 8.2 %collective-permute-start.6 = (bf16[128,576]{0,1:T(8,128)(2,1)S(1)}, bf16[128,576]{0,1:T(8,128)(2,1)S(1)}, u32[]{:S(2)}, u32[]{:S(2)}) collective-permute-start(bf16[128,576]{0,1:T(8,128)(2,1)S(1)} %copy-done.1), channel_id=1, source_target_pairs={{0,16},{8,24},{16,32},{24,40},{32,48},{40,56},{48,64},{56,72},{64,... | collective-permute-start | bytes 442376 | tf_op jit(solution)/shard_map/ppermute | solution.py:17
  73.5 5.4 %collective-permute-start.7 = (bf16[128,576]{0,1:T(8,128)(2,1)S(1)}, bf16[128,576]{0,1:T(8,128)(2,1)S(1)}, u32[]{:S(2)}, u32[]{:S(2)}) collective-permute-start(bf16[128,576]{0,1:T(8,128)(2,1)S(1)} %copy-done.1), channel_id=1, source_target_pairs={{0,8},{8,16},{16,24},{24,32},{32,40},{40,48},{48,56},{56,64},{64,7... | collective-permute-start | bytes 442376 | tf_op jit(solution)/shard_map/ppermute | solution.py:17
  79.6 11.8 %collective-permute-done.3 = bf16[128,576]{0,1:T(8,128)(2,1)S(1)} collective-permute-done((bf16[128,576]{0,1:T(8,128)(2,1)}, bf16[128,576]{0,1:T(8,128)(2,1)S(1)}, u32[]{:S(2)}, u32[]{:S(2)}) %collective-permute-start.3) | collective-permute-done | bytes 147488 | tf_op jit(solution)/shard_map/ppermute | solution.py:17
  92.7 15.1 %collective-permute-done.5 = bf16[128,576]{0,1:T(8,128)(2,1)S(1)} collective-permute-done((bf16[128,576]{0,1:T(8,128)(2,1)S(1)}, bf16[128,576]{0,1:T(8,128)(2,1)S(1)}, u32[]{:S(2)}, u32[]{:S(2)}) %collective-permute-start.5) | collective-permute-done | bytes 147488 | tf_op jit(solution)/shard_map/ppermute | solution.py:17
  108.5 6.1 %collective-permute-done.6 = bf16[128,576]{0,1:T(8,128)(2,1)S(1)} collective-permute-done((bf16[128,576]{0,1:T(8,128)(2,1)S(1)}, bf16[128,576]{0,1:T(8,128)(2,1)S(1)}, u32[]{:S(2)}, u32[]{:S(2)}) %collective-permute-start.6) | collective-permute-done | bytes 147488 | tf_op jit(solution)/shard_map/ppermute | solution.py:17
  119.1 6.8 %fusion.25 = (f32[8,128]{1,0:T(8,128)S(1)}, f32[8,128,1152]{1,2,0:T(8,128)}) fusion(pred[128,1152]{0,1:T(8,128)(4,1)S(1)} %compare_and_fusion, bf16[128,8,576]{0,2,1:T(8,128)(2,1)S(1)} %copy-done, bf16[1152,576]{0,1:T(8,128)(2,1)} %constant_dynamic-update-slice_fusion), kind=kOutput, calls=%fused_computation.47 | convolution fusion | flops 1364853888 | bytes 7376896 | tf_op jit(solution)/shard_map/sub | solution.py:28
  136.9 9.2 %collective-permute-start.15 = (f32[128,576]{0,1:T(8,128)S(1)}, f32[128,576]{0,1:T(8,128)S(1)}, u32[]{:S(2)}, u32[]{:S(2)}) collective-permute-start(f32[128,576]{0,1:T(8,128)S(1)} %get-tuple-element.3), channel_id=1, source_target_pairs={{64,0},{72,8},{80,16},{88,24},{96,32},{104,40},{112,48},{120,56},{... | collective-permute-start | bytes 884744 | tf_op jit(solution)/shard_map/ppermute | solution.py:17
  146.1 5.5 %collective-permute-start.14 = (f32[128,576]{0,1:T(8,128)S(1)}, f32[128,576]{0,1:T(8,128)S(1)}, u32[]{:S(2)}, u32[]{:S(2)}) collective-permute-start(f32[128,576]{0,1:T(8,128)S(1)} %get-tuple-element.4), channel_id=1, source_target_pairs={{56,0},{64,8},{72,16},{80,24},{88,32},{96,40},{104,48},{112,56},{1... | collective-permute-start | bytes 884744 | tf_op jit(solution)/shard_map/ppermute | solution.py:17
  155.7 8.4 %collective-permute-start.12 = (f32[128,576]{0,1:T(8,128)S(1)}, f32[128,576]{0,1:T(8,128)S(1)}, u32[]{:S(2)}, u32[]{:S(2)}) collective-permute-start(f32[128,576]{0,1:T(8,128)S(1)} %get-tuple-element.6), channel_id=1, source_target_pairs={{40,0},{48,8},{56,16},{64,24},{72,32},{80,40},{88,48},{96,56},{104... | collective-permute-start | bytes 884744 | tf_op jit(solution)/shard_map/ppermute | solution.py:17
  164.1 4.5 %collective-permute-start.11 = (f32[128,576]{0,1:T(8,128)S(1)}, f32[128,576]{0,1:T(8,128)S(1)}, u32[]{:S(2)}, u32[]{:S(2)}) collective-permute-start(f32[128,576]{0,1:T(8,128)S(1)} %get-tuple-element.7), channel_id=1, source_target_pairs={{32,0},{40,8},{48,16},{56,24},{64,32},{72,40},{80,48},{88,56},{96,... | collective-permute-start | bytes 884744 | tf_op jit(solution)/shard_map/ppermute | solution.py:17
  168.5 7.0 %collective-permute-done.15 = f32[128,576]{0,1:T(8,128)S(1)} collective-permute-done((f32[128,576]{0,1:T(8,128)S(1)}, f32[128,576]{0,1:T(8,128)S(1)}, u32[]{:S(2)}, u32[]{:S(2)}) %collective-permute-start.15) | collective-permute-done | bytes 294944 | tf_op jit(solution)/shard_map/ppermute | solution.py:17
  177.5 29.1 %collective-permute-done.14 = f32[128,576]{0,1:T(8,128)S(1)} collective-permute-done((f32[128,576]{0,1:T(8,128)S(1)}, f32[128,576]{0,1:T(8,128)S(1)}, u32[]{:S(2)}, u32[]{:S(2)}) %collective-permute-start.14) | collective-permute-done | bytes 294944 | tf_op jit(solution)/shard_map/ppermute | solution.py:17
  206.6 22.0 %collective-permute-start.9 = (f32[128,576]{0,1:T(8,128)S(1)}, f32[128,576]{0,1:T(8,128)S(1)}, u32[]{:S(2)}, u32[]{:S(2)}) collective-permute-start(f32[128,576]{0,1:T(8,128)S(1)} %get-tuple-element.9), channel_id=1, source_target_pairs={{16,0},{24,8},{32,16},{40,24},{48,32},{56,40},{64,48},{72,56},{80,... | collective-permute-start | bytes 884744 | tf_op jit(solution)/shard_map/ppermute | solution.py:17
  228.7 26.3 %collective-permute-done.13 = f32[128,576]{0,1:T(8,128)S(1)} collective-permute-done((f32[128,576]{0,1:T(8,128)S(1)}, f32[128,576]{0,1:T(8,128)S(1)}, u32[]{:S(2)}, u32[]{:S(2)}) %collective-permute-start.13) | collective-permute-done | bytes 294944 | tf_op jit(solution)/shard_map/ppermute | solution.py:17
  260.9 24.9 %collective-permute-done.12 = f32[128,576]{0,1:T(8,128)S(1)} collective-permute-done((f32[128,576]{0,1:T(8,128)S(1)}, f32[128,576]{0,1:T(8,128)S(1)}, u32[]{:S(2)}, u32[]{:S(2)}) %collective-permute-start.12) | collective-permute-done | bytes 294944 | tf_op jit(solution)/shard_map/ppermute | solution.py:17
  285.8 25.1 %collective-permute-done.11 = f32[128,576]{0,1:T(8,128)S(1)} collective-permute-done((f32[128,576]{0,1:T(8,128)S(1)}, f32[128,576]{0,1:T(8,128)S(1)}, u32[]{:S(2)}, u32[]{:S(2)}) %collective-permute-start.11) | collective-permute-done | bytes 294944 | tf_op jit(solution)/shard_map/ppermute | solution.py:17
  311.0 17.8 %collective-permute-done.10 = f32[128,576]{0,1:T(8,128)S(1)} collective-permute-done((f32[128,576]{0,1:T(8,128)S(1)}, f32[128,576]{0,1:T(8,128)S(1)}, u32[]{:S(2)}, u32[]{:S(2)}) %collective-permute-start.10) | collective-permute-done | bytes 294944 | tf_op jit(solution)/shard_map/ppermute | solution.py:17
  328.7 12.5 %collective-permute-done.9 = f32[128,576]{0,1:T(8,128)S(1)} collective-permute-done((f32[128,576]{0,1:T(8,128)S(1)}, f32[128,576]{0,1:T(8,128)S(1)}, u32[]{:S(2)}, u32[]{:S(2)}) %collective-permute-start.9) | collective-permute-done | bytes 294944 | tf_op jit(solution)/shard_map/ppermute | solution.py:17
  341.2 6.3 %collective-permute-done.8 = f32[128,576]{0,1:T(8,128)S(1)} collective-permute-done((f32[128,576]{0,1:T(8,128)S(1)}, f32[128,576]{0,1:T(8,128)S(1)}, u32[]{:S(2)}, u32[]{:S(2)}) %collective-permute-start.8) | collective-permute-done | bytes 294944 | tf_op jit(solution)/shard_map/ppermute | solution.py:17
  347.7 29.4 %all-reduce.3 = bf16[128,576]{0,1:T(8,128)(2,1)} all-reduce(f32[128,576]{0,1:T(8,128)S(1)} %fusion.20), channel_id=1, replica_groups=mesh['ctx'=64,'head'=8] {'head'}, use_global_device_ids=true, to_apply=%region_3.4 | all-reduce | flops 73728 | bytes 442368 | tf_op jit(solution)/shard_map/psum | solution.py:75
  (37 shorter events, 46.4 us)
Async XLA Ops:
  0.6 118.4 %copy-start = (bf16[128,8,576]{0,2,1:T(8,128)(2,1)S(1)}, bf16[128,8,576]{0,2,1:T(8,128)(2,1)}, u32[]{:S(2)}) copy-start(bf16[128,8,576]{0,2,1:T(8,128)(2,1)} %param.4) | copy-start | bytes 3538948
  0.6 43.2 %copy-start.1 = (bf16[128,576]{0,1:T(8,128)(2,1)S(1)}, bf16[128,576]{0,1:T(8,128)(2,1)}, u32[]{:S(2)}) copy-start(bf16[128,576]{0,1:T(8,128)(2,1)} %param.5) | copy-start | bytes 442372
  0.7 43.1 %collective-permute-start = (bf16[128,576]{0,1:T(8,128)(2,1)}, bf16[128,576]{0,1:T(8,128)(2,1)S(1)}, u32[]{:S(2)}, u32[]{:S(2)}) collective-permute-start(bf16[128,576]{0,1:T(8,128)(2,1)} %param.5), channel_id=1, source_target_pairs={{0,64},{8,72},{16,80},{24,88},{32,96},{40,104},{48,112},{56,120},{... | collective-permute-start | bytes 442376 | tf_op jit(solution)/shard_map/ppermute | solution.py:17
  16.5 48.1 %collective-permute-start.1 = (bf16[128,576]{0,1:T(8,128)(2,1)}, bf16[128,576]{0,1:T(8,128)(2,1)S(1)}, u32[]{:S(2)}, u32[]{:S(2)}) collective-permute-start(bf16[128,576]{0,1:T(8,128)(2,1)} %param.5), channel_id=1, source_target_pairs={{0,56},{8,64},{16,72},{24,80},{32,88},{40,96},{48,104},{56,112},{6... | collective-permute-start | bytes 442376 | tf_op jit(solution)/shard_map/ppermute | solution.py:17
  22.2 51.3 %collective-permute-start.2 = (bf16[128,576]{0,1:T(8,128)(2,1)}, bf16[128,576]{0,1:T(8,128)(2,1)S(1)}, u32[]{:S(2)}, u32[]{:S(2)}) collective-permute-start(bf16[128,576]{0,1:T(8,128)(2,1)} %param.5), channel_id=1, source_target_pairs={{0,48},{8,56},{16,64},{24,72},{32,80},{40,88},{48,96},{56,104},{64... | collective-permute-start | bytes 442376 | tf_op jit(solution)/shard_map/ppermute | solution.py:17
  26.5 64.8 %collective-permute-start.3 = (bf16[128,576]{0,1:T(8,128)(2,1)}, bf16[128,576]{0,1:T(8,128)(2,1)S(1)}, u32[]{:S(2)}, u32[]{:S(2)}) collective-permute-start(bf16[128,576]{0,1:T(8,128)(2,1)} %param.5), channel_id=1, source_target_pairs={{0,40},{8,48},{16,56},{24,64},{32,72},{40,80},{48,88},{56,96},{64,... | collective-permute-start | bytes 442376 | tf_op jit(solution)/shard_map/ppermute | solution.py:17
  35.2 56.9 %collective-permute-start.4 = (bf16[128,576]{0,1:T(8,128)(2,1)}, bf16[128,576]{0,1:T(8,128)(2,1)S(1)}, u32[]{:S(2)}, u32[]{:S(2)}) collective-permute-start(bf16[128,576]{0,1:T(8,128)(2,1)} %param.5), channel_id=1, source_target_pairs={{0,32},{8,40},{16,48},{24,56},{32,64},{40,72},{48,80},{56,88},{64,... | collective-permute-start | bytes 442376 | tf_op jit(solution)/shard_map/ppermute | solution.py:17
  43.8 64.0 %collective-permute-start.5 = (bf16[128,576]{0,1:T(8,128)(2,1)S(1)}, bf16[128,576]{0,1:T(8,128)(2,1)S(1)}, u32[]{:S(2)}, u32[]{:S(2)}) collective-permute-start(bf16[128,576]{0,1:T(8,128)(2,1)S(1)} %copy-done.1), channel_id=1, source_target_pairs={{0,24},{8,32},{16,40},{24,48},{32,56},{40,64},{48,72},{56,80},{64,... | collective-permute-start | bytes 442376 | tf_op jit(solution)/shard_map/ppermute | solution.py:17
  64.6 50.1 %collective-permute-start.6 = (bf16[128,576]{0,1:T(8,128)(2,1)S(1)}, bf16[128,576]{0,1:T(8,128)(2,1)S(1)}, u32[]{:S(2)}, u32[]{:S(2)}) collective-permute-start(bf16[128,576]{0,1:T(8,128)(2,1)S(1)} %copy-done.1), channel_id=1, source_target_pairs={{0,16},{8,24},{16,32},{24,40},{32,48},{40,56},{48,64},{56,72},{64,... | collective-permute-start | bytes 442376 | tf_op jit(solution)/shard_map/ppermute | solution.py:17
  73.5 44.2 %collective-permute-start.7 = (bf16[128,576]{0,1:T(8,128)(2,1)S(1)}, bf16[128,576]{0,1:T(8,128)(2,1)S(1)}, u32[]{:S(2)}, u32[]{:S(2)}) collective-permute-start(bf16[128,576]{0,1:T(8,128)(2,1)S(1)} %copy-done.1), channel_id=1, source_target_pairs={{0,8},{8,16},{16,24},{24,32},{32,40},{40,48},{48,56},{56,64},{64,7... | collective-permute-start | bytes 442376 | tf_op jit(solution)/shard_map/ppermute | solution.py:17
  125.8 4.4 %copy-start.2 = (f32[8,128,1152]{1,2,0:T(8,128)S(1)}, f32[8,128,1152]{1,2,0:T(8,128)}, u32[]{:S(2)}) copy-start(f32[8,128,1152]{1,2,0:T(8,128)} %get-tuple-element.11) | copy-start | bytes 14155780
  136.9 38.7 %collective-permute-start.15 = (f32[128,576]{0,1:T(8,128)S(1)}, f32[128,576]{0,1:T(8,128)S(1)}, u32[]{:S(2)}, u32[]{:S(2)}) collective-permute-start(f32[128,576]{0,1:T(8,128)S(1)} %get-tuple-element.3), channel_id=1, source_target_pairs={{64,0},{72,8},{80,16},{88,24},{96,32},{104,40},{112,48},{120,56},{... | collective-permute-start | bytes 884744 | tf_op jit(solution)/shard_map/ppermute | solution.py:17
  146.1 60.5 %collective-permute-start.14 = (f32[128,576]{0,1:T(8,128)S(1)}, f32[128,576]{0,1:T(8,128)S(1)}, u32[]{:S(2)}, u32[]{:S(2)}) collective-permute-start(f32[128,576]{0,1:T(8,128)S(1)} %get-tuple-element.4), channel_id=1, source_target_pairs={{56,0},{64,8},{72,16},{80,24},{88,32},{96,40},{104,48},{112,56},{1... | collective-permute-start | bytes 884744 | tf_op jit(solution)/shard_map/ppermute | solution.py:17
  151.6 103.3 %collective-permute-start.13 = (f32[128,576]{0,1:T(8,128)S(1)}, f32[128,576]{0,1:T(8,128)S(1)}, u32[]{:S(2)}, u32[]{:S(2)}) collective-permute-start(f32[128,576]{0,1:T(8,128)S(1)} %get-tuple-element.5), channel_id=1, source_target_pairs={{48,0},{56,8},{64,16},{72,24},{80,32},{88,40},{96,48},{104,56},{11... | collective-permute-start | bytes 884744 | tf_op jit(solution)/shard_map/ppermute | solution.py:17
  155.7 130.2 %collective-permute-start.12 = (f32[128,576]{0,1:T(8,128)S(1)}, f32[128,576]{0,1:T(8,128)S(1)}, u32[]{:S(2)}, u32[]{:S(2)}) collective-permute-start(f32[128,576]{0,1:T(8,128)S(1)} %get-tuple-element.6), channel_id=1, source_target_pairs={{40,0},{48,8},{56,16},{64,24},{72,32},{80,40},{88,48},{96,56},{104... | collective-permute-start | bytes 884744 | tf_op jit(solution)/shard_map/ppermute | solution.py:17
  164.1 146.9 %collective-permute-start.11 = (f32[128,576]{0,1:T(8,128)S(1)}, f32[128,576]{0,1:T(8,128)S(1)}, u32[]{:S(2)}, u32[]{:S(2)}) collective-permute-start(f32[128,576]{0,1:T(8,128)S(1)} %get-tuple-element.7), channel_id=1, source_target_pairs={{32,0},{40,8},{48,16},{56,24},{64,32},{72,40},{80,48},{88,56},{96,... | collective-permute-start | bytes 884744 | tf_op jit(solution)/shard_map/ppermute | solution.py:17
  175.6 153.1 %collective-permute-start.10 = (f32[128,576]{0,1:T(8,128)S(1)}, f32[128,576]{0,1:T(8,128)S(1)}, u32[]{:S(2)}, u32[]{:S(2)}) collective-permute-start(f32[128,576]{0,1:T(8,128)S(1)} %get-tuple-element.8), channel_id=1, source_target_pairs={{24,0},{32,8},{40,16},{48,24},{56,32},{64,40},{72,48},{80,56},{88,... | collective-permute-start | bytes 884744 | tf_op jit(solution)/shard_map/ppermute | solution.py:17
  206.6 134.5 %collective-permute-start.9 = (f32[128,576]{0,1:T(8,128)S(1)}, f32[128,576]{0,1:T(8,128)S(1)}, u32[]{:S(2)}, u32[]{:S(2)}) collective-permute-start(f32[128,576]{0,1:T(8,128)S(1)} %get-tuple-element.9), channel_id=1, source_target_pairs={{16,0},{24,8},{32,16},{40,24},{48,32},{56,40},{64,48},{72,56},{80,... | collective-permute-start | bytes 884744 | tf_op jit(solution)/shard_map/ppermute | solution.py:17
  254.9 92.6 %collective-permute-start.8 = (f32[128,576]{0,1:T(8,128)S(1)}, f32[128,576]{0,1:T(8,128)S(1)}, u32[]{:S(2)}, u32[]{:S(2)}) collective-permute-start(f32[128,576]{0,1:T(8,128)S(1)} %get-tuple-element.2), channel_id=1, source_target_pairs={{8,0},{16,8},{24,16},{32,24},{40,32},{48,40},{56,48},{64,56},{72,6... | collective-permute-start | bytes 884744 | tf_op jit(solution)/shard_map/ppermute | solution.py:17
where the time goes:
time: 378 us; the launch traced here: 377 us
  waiting for transfers between devices  203 us (54%)
  starting transfers between devices  112 us (30%)
  blocking collectives  29.4 us (8%)
  matrix products  21.6 us (6%)
  local copies, waits for them, and re-layouts  9.14 us (2%)
    ppermute x16, waiting for transfers between devices, passed_along(): lax.ppermute(value, axis, [(source, source + steps) for source in range(l...  203 us
    ppermute x16, starting transfers between devices, passed_along(): lax.ppermute(value, axis, [(source, source + steps) for source in range(l...  112 us
    psum x1, blocking collectives, on_device(): owned = lax.psum(return_owned(grad_keys, tok_rows), 'head')  29.4 us
  transfers between devices with their start and end apart: 16, of which 13 were waited for; matrix products, arithmetic and copies ran while one was open for 3% of the time, Pallas kernels for 0%

commit v1 on v0

v1 whole, which is shorter than its diff:
```python
import functools

import jax
import jax.numpy as jnp
from jax import lax
from jax.experimental import pallas as pl
from jax.experimental.pallas import tpu as pltpu
from jax.sharding import PartitionSpec as P

LAT_C = 512
SPAN = 8
LANES = 256

score_scale = 192.0 ** (-0.5)
exp2_scale = score_scale * 1.4426950408889634
HIDDEN = -1e30
MESH = pl.DeviceIdType.MESH
NT = (((1,), (1,)), ((), ()))
TN = (((0,), (0,)), ((), ()))


def schedule(span):
    order = []
    for k in range(span, -1, -2):
        order.append(("D", k))
        order.append(("A", k))
        if k > 0:
            order.append(("A", k - 1))
        if k + 2 <= span:
            order.append(("B", k + 2))
            order.append(("B", k + 1))
        if k + 4 <= span:
            order.append(("C", span - (span - k - 4) // 2))
    last = span % 2
    order.append(("B", last))
    if last == 1:
        order.append(("B", 0))
    done = [k for op, k in order if op == "C"]
    rest = [k for k in range(span, -1, -1) if k not in done]
    for n, k in enumerate(rest):
        order.append(("C", k))
        order.append(("Q", n))
    return order


def kernel(
    span, nctx, nhead,
    doc_ref, q_hbm, g_hbm, lat_hbm, gq_hbm, gl_hbm,
    kwin, q, g, ew, gp, pw, ds, starts, tops, part, csend, crecv, xsend, xrecv, zsend, zrecv, gqbuf, glbuf,
    local, gz_s, gz_r, gx_s, gx_r, gc_s, gc_r, rc_s, rc_r, rx_s, rx_r, rz_s, rz_r, ag_s, ag_r,
):
    tok = lat_hbm.shape[0]
    rows = q_hbm.shape[0]
    heads = rows // tok
    half, piece, nx = tok // 2, tok // nhead, nhead // 2
    chunks = rows // LANES
    s = lax.axis_index("ctx")
    hd = lax.axis_index("head")
    x, c = hd // 2, lax.rem(hd, 2)
    right, left = lax.rem(s + 1, nctx), lax.rem(s + nctx - 1, nctx)
    mine = c * half + x * piece

    def xpeer(j):
        return lax.rem(x + j, nx)

    loads = [
        pltpu.make_async_copy(lat_hbm, kwin.at[pl.ds(0, tok)], local.at[0]),
        pltpu.make_async_copy(q_hbm, q, local.at[1]),
        pltpu.make_async_copy(g_hbm, g, local.at[2]),
    ]
    for load in loads:
        load.start()

    barrier = pltpu.get_barrier_semaphore()
    peers = [(right, hd), (left, hd)] + [(s, lax.rem(hd + j, nhead)) for j in range(1, nhead)]
    for peer in peers:
        pl.semaphore_signal(barrier, inc=1, device_id=peer, device_id_type=MESH)
    pl.semaphore_wait(barrier, len(peers))

    def remote(src, dst, send, recv, dev):
        return pltpu.make_async_remote_copy(
            src_ref=src, dst_ref=dst, send_sem=send, recv_sem=recv, device_id=dev, device_id_type=MESH
        )

    def rows_at(block, start, count):
        return pl.ds(pl.multiple_of(block * tok + start, 16), count)

    sent = []

    def go(copy):
        copy.start()
        sent.append(copy)

    def g_z(k):
        src = lat_hbm.at[rows_at(0, mine, piece)] if k == 1 else kwin.at[rows_at(k - 1, mine, piece)]
        return remote(src, kwin.at[rows_at(k, mine, piece)], gz_s.at[k - 1], gz_r.at[k - 1], (right, hd))

    def g_x(k, j):
        ref = kwin.at[rows_at(k, mine, piece)]
        return remote(ref, ref, gx_s.at[(k - 1) * (nx - 1) + j - 1], gx_r.at[(k - 1) * (nx - 1) + j - 1], (s, xpeer(j) * 2 + c))

    def g_c(k):
        ref = kwin.at[rows_at(k, c * half, half)]
        return remote(ref, ref, gc_s.at[k - 1], gc_r.at[k - 1], (s, x * 2 + 1 - c))

    go(g_z(1))

    doc = doc_ref[pl.ds(s, 1), :] - (s - span) * tok
    halves = lax.broadcasted_iota(jnp.int32, (16, tok), 0) == 0
    coded = jnp.where(halves, lax.shift_right_arithmetic(doc, 5), doc & 31).astype(jnp.float32).astype(jnp.bfloat16)
    spread = (
        lax.shift_right_logical(lax.broadcasted_iota(jnp.int32, (tok, rows), 1), heads.bit_length() - 1)
        == lax.broadcasted_iota(jnp.int32, (tok, rows), 0)
    )
    spread = jnp.where(spread, 1.0, 0.0).astype(jnp.bfloat16)
    coded = jnp.dot(coded, spread, preferred_element_type=jnp.float32)
    starts[...] = coded[0:1, :] * 32.0 + coded[1:2, :]

    for load in loads:
        load.wait()

    def scores(k):
        def chunk(n, _):
            at = pl.ds(pl.multiple_of(n * LANES, LANES), LANES)
            here = pl.ds(k * tok, tok)
            score = lax.dot_general(kwin[here, :], q[at, :], NT, preferred_element_type=jnp.float32)
            grad = lax.dot_general(kwin[here, :LAT_C], g[at, :], NT, preferred_element_type=jnp.float32)
            row = lax.broadcasted_iota(jnp.int32, (tok, LANES), 0)
            seen = (row + (span - k) * tok).astype(jnp.float32) >= starts[:, at]
            if k == 0:
                lane = lax.broadcasted_iota(jnp.int32, (tok, LANES), 1) + n * LANES
                seen = seen & (row <= lax.shift_right_logical(lane, heads.bit_length() - 1))
            score = jnp.where(seen, score, HIDDEN)
            top = jnp.max(score, axis=0, keepdims=True)
            if k > 0:
                before = tops[k - 1 : k, at]
                top = jnp.maximum(top, before)
            expo = jnp.exp2((score - top) * exp2_scale)
            total = jnp.sum(expo, axis=0, keepdims=True)
            if k > 0:
                total = total + tops[span + 1 : span + 2, at] * jnp.exp2((before - top) * exp2_scale)
            tops[k : k + 1, at] = top
            tops[span + 1 : span + 2, at] = total
            ew[here, at] = expo
            gp[here, at] = grad
            return 0

        lax.fori_loop(0, chunks, chunk, 0)

    scores(0)
    for t in range(1, span + 3):
        if t <= span:
            g_z(t).wait_recv()
            if t < span:
                go(g_z(t + 1))
            for j in range(1, nx):
                go(g_x(t, j))
        if 2 <= t <= span + 1:
            for j in range(1, nx):
                g_x(t - 1, j).wait_recv()
            go(g_c(t - 1))
        if t >= 3:
            g_c(t - 2).wait_recv()
            scores(t - 2)

    def soften(n, _):
        at = pl.ds(pl.multiple_of(n * LANES, LANES), LANES)
        over = 1.0 / tops[span + 1 : span + 2, at]
        final = tops[span : span + 1, at]
        delta = jnp.zeros((1, LANES), jnp.float32)
        for k in range(span + 1):
            here = pl.ds(k * tok, tok)
            weight = ew[here, at] * (jnp.exp2((tops[k : k + 1, at] - final) * exp2_scale) * over)
            prob = weight.astype(jnp.bfloat16)
            pw[here, at] = prob
            ew[here, at] = weight
            delta = delta + jnp.sum(prob.astype(jnp.float32) * gp[here, at], axis=0, keepdims=True)
        for k in range(span + 1):
            here = pl.ds(k * tok, tok)
            ds[here, at] = (ew[here, at] * (gp[here, at] - delta) * score_scale).astype(jnp.bfloat16)
        return 0

    lax.fori_loop(0, chunks, soften, 0)

    def products(k):
        low = max(k - 1, 0)
        here = pl.ds(low * tok, (k + 1 - low) * tok)
        part[here, :] = jnp.dot(ds[here, :], q[...], preferred_element_type=jnp.float32)
        part[here, :LAT_C] += jnp.dot(pw[here, :], g[...], preferred_element_type=jnp.float32)

    def r_c(k):
        at = pl.ds(k * half, half)
        return remote(csend.at[at], crecv.at[at], rc_s.at[k], rc_r.at[k], (s, x * 2 + 1 - c))

    def r_x(k, j):
        src = xsend.at[pl.ds(pl.multiple_of(k * half + xpeer(j) * piece, 16), piece)]
        dst = xrecv.at[pl.ds((k * (nx - 1) + j - 1) * piece, piece)]
        return remote(src, dst, rx_s.at[k * (nx - 1) + j - 1], rx_r.at[k * (nx - 1) + j - 1], (s, xpeer(j) * 2 + c))

    def r_z(k):
        at = pl.ds((k - 1) * piece, piece)
        return remote(zsend.at[at], zrecv.at[at], rz_s.at[k - 1], rz_r.at[k - 1], (left, hd))

    outs = []

    def ag(j):
        ref = glbuf.at[rows_at(0, mine, piece)]
        return remote(ref, ref, ag_s.at[j - 1], ag_r.at[j - 1], (s, lax.rem(hd + j, nhead)))

    for op, k in schedule(span):
        if op == "D":
            products(k)
        elif op == "A":
            csend[pl.ds(k * half, half), :] = part[rows_at(k, (1 - c) * half, half), :].astype(jnp.bfloat16)
            go(r_c(k))
        elif op == "B":
            r_c(k).wait_recv()
            total = part[rows_at(k, c * half, half), :] + crecv[pl.ds(k * half, half), :].astype(jnp.float32)
            part[rows_at(k, c * half, half), :] = total
            xsend[pl.ds(k * half, half), :] = total.astype(jnp.bfloat16)
            for j in range(1, nx):
                go(r_x(k, j))
        elif op == "C":
            total = part[rows_at(k, mine, piece), :]
            for j in range(1, nx):
                r_x(k, j).wait_recv()
                total = total + xrecv[pl.ds((k * (nx - 1) + j - 1) * piece, piece), :].astype(jnp.float32)
            if k < span:
                r_z(k + 1).wait_recv()
                total = total + zrecv[pl.ds(k * piece, piece), :].astype(jnp.float32)
            if k > 0:
                zsend[pl.ds((k - 1) * piece, piece), :] = total.astype(zsend.dtype)
                go(r_z(k))
            else:
                glbuf[rows_at(0, mine, piece), :] = total.astype(jnp.bfloat16)
                for j in range(1, nhead):
                    go(ag(j))
        elif k < chunks:
            at = pl.ds(k * LANES, LANES)
            gqbuf[at, :] = lax.dot_general(ds[:, at], kwin[...], TN, preferred_element_type=jnp.float32).astype(jnp.bfloat16)
            out = pltpu.make_async_copy(gqbuf.at[at], gq_hbm.at[at], local.at[3 + k])
            out.start()
            outs.append(out)

    for j in range(1, nhead):
        ag(j).wait_recv()
    last = pltpu.make_async_copy(glbuf, gl_hbm, local.at[0])
    last.start()
    for copy in sent:
        copy.wait_send()
    for out in outs:
        out.wait()
    last.wait()


def on_device(nctx, nhead, span, queries, latents, grad_out, doc_ids):
    tok, heads, lat = queries.shape
    rows = tok * heads
    window = (span + 1) * tok
    piece, nx = tok // nhead, nhead // 2
    bf16, f32 = jnp.bfloat16, jnp.float32
    dma = pltpu.SemaphoreType.DMA
    grad_queries, grad_latents = pl.pallas_call(
        functools.partial(kernel, span, nctx, nhead),
        out_shape=(
            jax.ShapeDtypeStruct((rows, lat), bf16),
            jax.ShapeDtypeStruct((tok, lat), bf16),
        ),
        in_specs=[pl.BlockSpec(memory_space=pltpu.VMEM)] + [pl.BlockSpec(memory_space=pl.ANY)] * 3,
        out_specs=(pl.BlockSpec(memory_space=pl.ANY), pl.BlockSpec(memory_space=pl.ANY)),
        scratch_shapes=[
            pltpu.VMEM((window, lat), bf16),
            pltpu.VMEM((rows, lat), bf16),
            pltpu.VMEM((rows, LAT_C), bf16),
            pltpu.VMEM((window, rows), f32),
            pltpu.VMEM((window, rows), f32),
            pltpu.VMEM((window, rows), bf16),
            pltpu.VMEM((window, rows), bf16),
            pltpu.VMEM((1, rows), f32),
            pltpu.VMEM((span + 2, rows), f32),
            pltpu.VMEM((window, lat), f32),
            pltpu.VMEM(((span + 1) * tok // 2, lat), bf16),
            pltpu.VMEM(((span + 1) * tok // 2, lat), bf16),
            pltpu.VMEM(((span + 1) * tok // 2, lat), bf16),
            pltpu.VMEM(((span + 1) * (nx - 1) * piece, lat), bf16),
            pltpu.VMEM((span * piece, lat), f32),
            pltpu.VMEM((span * piece, lat), f32),
            pltpu.VMEM((rows, lat), bf16),
            pltpu.VMEM((tok, lat), bf16),
            dma((3 + rows // LANES,)),
            dma((span,)), dma((span,)),
            dma((span * (nx - 1),)), dma((span * (nx - 1),)),
            dma((span,)), dma((span,)),
            dma((span + 1,)), dma((span + 1,)),
            dma(((span + 1) * (nx - 1),)), dma(((span + 1) * (nx - 1),)),
            dma((span,)), dma((span,)),
            dma((nhead - 1,)), dma((nhead - 1,)),
        ],
        compiler_params=pltpu.CompilerParams(
            collective_id=0, has_side_effects=True, vmem_limit_bytes=48 * 1024 * 1024
        ),
    )(doc_ids.reshape(nctx, tok), queries.reshape(rows, lat), grad_out.reshape(rows, LAT_C), latents)
    return grad_queries.reshape(queries.shape), grad_latents


def solution(mesh):
    nctx, nhead = mesh.shape["ctx"], mesh.shape["head"]
    placed = (P("ctx", "head", None), P("ctx", None), P("ctx", "head", None), P())
    return jax.shard_map(
        functools.partial(on_device, nctx, nhead, SPAN),
        mesh=mesh,
        in_specs=placed,
        out_specs=(P("ctx", "head", None), P("ctx", None)),
        check_vma=False,
    )
```

time: 378 us -> 93 us (0.25)
  the two profiles are of different devices: /device:TPU:16 before, /device:TPU:1 now
where the time goes in v1:
time: 93 us; the launch traced here: 92.8 us
  Pallas kernels  85 us (91%)
  local copies, waits for them, and re-layouts  7.07 us (8%)
    pallas_call x1, Pallas kernels, on_device(): pl.pallas_call(functools.partial(kernel, span, nctx, nhead), out_shape=(j...  85 us
    unnamed x8, local copies, waits for them, and re-layouts  7.07 us

profile of v1, /device:TPU:1, one launch (start us, length us, event | category | flops | bytes accessed | tf_op | source)
XLA Modules:
  0.0 92.8 jit_solution(17237395991373693774)
XLA Ops:
  0.6 1.1 %copy.7.lat_hbm = bf16[128,576]{1,0:T(8,128)(2,1)S(1)} copy(bf16[128,576]{0,1:T(8,128)(2,1)} %param.5) | data formatting | bytes 294912 | tf_op args[1]
  1.7 0.0 copy-start.1
  1.7 2.2 %copy.6 = bf16[128,8,576]{2,1,0:T(8,128)(2,1)S(1)} copy(bf16[128,8,576]{0,2,1:T(8,128)(2,1)} %param.4) | data formatting | bytes 2359296 | tf_op args[0]
  3.9 0.0 copy-done.1
  3.9 0.0 copy-start
  3.9 1.2 %copy-done = bf16[128,8,512]{2,1,0:T(8,128)(2,1)S(1)} copy-done((bf16[128,8,512]{2,1,0:T(8,128)(2,1)S(1)}, bf16[128,8,512]{2,1,0:T(8,128)(2,1)}, u32[]{:S(2)}) %copy-start) | copy-done | bytes 1048600
  5.2 85.0 %shard_map.59 = (bf16[1024,576]{1,0:T(8,128)(2,1)S(1)}, bf16[128,576]{1,0:T(8,128)(2,1)S(1)}) custom-call(s32[64,128]{1,0:T(8,128)S(1)} %bitcast.7, bf16[1024,576]{1,0:T(8,128)(2,1)S(1)} %bitcast.4, bf16[1024,512]{1,0:T(8,128)(2,1)S(1)} %bitcast.6, bf16[128,576]{1,0:T(8,128)(2,1)S(1)} %copy.7.lat_hbm), custom_call_target="tpu_custom_call" | custom-call | tf_op jit(solution)/shard_map/pallas_call | solution.py:263
  90.2 1.8 %copy.8 = bf16[128,8,576]{0,2,1:T(8,128)(2,1)} copy(bf16[128,8,576]{2,1,0:T(8,128)(2,1)S(1)} %bitcast.5) | data formatting | bytes 2359296
  92.0 0.8 copy.9
Async XLA Ops:
  1.7 2.2 %copy-start.1 = (s32[8192]{0:T(1024)S(1)}, s32[8192]{0:T(1024)}, u32[]{:S(2)}) copy-start(s32[8192]{0:T(1024)} %param.7) | copy-start | bytes 98308
  3.9 1.2 %copy-start = (bf16[128,8,512]{2,1,0:T(8,128)(2,1)S(1)}, bf16[128,8,512]{2,1,0:T(8,128)(2,1)}, u32[]{:S(2)}) copy-start(bf16[128,8,512]{2,1,0:T(8,128)(2,1)} %param.6) | copy-start | bytes 3145732

commit v2 on v0

v2 whole, which is shorter than its diff:
```python
import functools

import jax
import jax.numpy as jnp
from jax import lax
from jax.experimental import pallas as pl
from jax.experimental.pallas import tpu as pltpu
from jax.sharding import PartitionSpec as P

LAT_C = 512
SPAN = 8
LANES = 128
SC_HEADS = 4
SOFT_HEADS = 2
Q_HEADS = 2

score_scale = 192.0 ** (-0.5)
exp2_scale = score_scale * 1.4426950408889634
HIDDEN = -1e30
MESH = pl.DeviceIdType.MESH
NT = (((1,), (1,)), ((), ()))

STRAIGHT = (6, 3, 2, 1)
RELAYED = {3: (5, 4), 6: (8, 7)}
GROUPS = ((1, 2), (3, 1), (6, 1), (4, 2), (7, 2))
BACK = ((7, 2), (4, 2), (6, 1), (3, 1), (1, 2), (0, 1))


def kernel(
    span, nctx, nhead,
    doc_ref, q_hbm, g_hbm, lat_hbm, gq_hbm, gl_hbm,
    kwin, kt, q, graw, gf, g, ew, gp, pw, ds, tops, part, csend, crecv, xsend, xrecv, zsend, zrecv, gqbuf, glbuf,
    local, gz_s, gz_r, gx_s, gx_r, gc_s, gc_r, rc_s, rc_r, rx_s, rx_r, rz_s, rz_r, ag_s, ag_r,
):
    heads, lat, tok = q_hbm.shape
    rows = heads * tok
    half, piece, nx = tok // 2, tok // nhead, nhead // 2
    s = lax.axis_index("ctx")
    hd = lax.axis_index("head")
    x, c = hd // 2, lax.rem(hd, 2)
    mine = pl.multiple_of(c * half + x * piece, 16)

    def xpeer(j):
        return lax.rem(x + j, nx)

    def ctx(step):
        return lax.rem(s + step + nctx, nctx)

    barrier = pltpu.get_barrier_semaphore()
    peers = [(s, lax.rem(hd + j, nhead)) for j in range(1, nhead)]
    for step in STRAIGHT:
        peers += [(ctx(step), hd), (ctx(-step), hd)]
    for peer in peers:
        pl.semaphore_signal(barrier, inc=1, device_id=peer, device_id_type=MESH)

    loads = [pltpu.make_async_copy(lat_hbm, kt.at[:, pl.ds(0, tok)], local.at[0])]
    loads += [pltpu.make_async_copy(g_hbm, graw, local.at[1])]
    loads += [pltpu.make_async_copy(q_hbm.at[h], q.at[:, pl.ds(h * tok, tok)], local.at[2 + h]) for h in range(heads)]
    for load in loads:
        load.start()

    def remote(src, dst, send, recv, dev):
        return pltpu.make_async_remote_copy(
            src_ref=src, dst_ref=dst, send_sem=send, recv_sem=recv, device_id=dev, device_id_type=MESH
        )

    sent = []

    def go(copy):
        copy.start()
        sent.append(copy)

    def g_z(k, step):
        src = kwin.at[k - step, pl.ds(mine, piece)]
        return remote(src, kwin.at[k, pl.ds(mine, piece)], gz_s.at[k - 1], gz_r.at[k - 1], (ctx(step), hd))

    def g_x(n, j):
        ref = kwin.at[pl.ds(*GROUPS[n]), pl.ds(mine, piece)]
        at = n * (nx - 1) + j - 1
        return remote(ref, ref, gx_s.at[at], gx_r.at[at], (s, xpeer(j) * 2 + c))

    def g_c(n):
        ref = kwin.at[pl.ds(*GROUPS[n]), pl.ds(pl.multiple_of(c * half, 16), half)]
        return remote(ref, ref, gc_s.at[n], gc_r.at[n], (s, x * 2 + 1 - c))

    start = doc_ref[pl.ds(s, 1), :] - (s - span) * tok

    def scores(k, count):
        height = count * tok
        width = SC_HEADS * tok
        starts = jnp.concatenate([start] * SC_HEADS, axis=1)
        keys = kwin[k : k + count].reshape(height, lat)
        row = lax.broadcasted_iota(jnp.int32, (height, width), 0)
        place = row + (span - k) * tok
        if count == 2:
            place = jnp.where(row < tok, place, place - 2 * tok)
        seen = place >= starts
        if k == 0:
            token = lax.broadcasted_iota(jnp.int32, (height, tok), 1)
            seen = seen & (row <= jnp.concatenate([token] * SC_HEADS, axis=1))
        here = pl.ds(k * tok, height)

        def chunk(n, _):
            at = pl.ds(pl.multiple_of(n * width, width), width)
            score = jnp.dot(keys, q[:, at], preferred_element_type=jnp.float32)
            grad = lax.dot_general(keys[:, :LAT_C], g[at, :], NT, preferred_element_type=jnp.float32)
            score = jnp.where(seen, score, HIDDEN)
            top = jnp.max(score, axis=0, keepdims=True)
            if k > 0:
                before = tops[span + 2 : span + 3, at]
                top = jnp.maximum(top, before)
            expo = jnp.exp2((score - top) * exp2_scale)
            total = jnp.sum(expo, axis=0, keepdims=True)
            if k > 0:
                total = total + tops[span + 1 : span + 2, at] * jnp.exp2((before - top) * exp2_scale)
            for extra in range(count):
                tops[k + extra : k + extra + 1, at] = top
            tops[span + 1 : span + 2, at] = total
            tops[span + 2 : span + 3, at] = top
            ew[here, at] = expo
            gp[here, at] = grad
            return 0

        lax.fori_loop(0, heads // SC_HEADS, chunk, 0)

    def turn(k):
        kt[:, pl.ds(k * tok, tok)] = kwin[k].T

    loads[0].wait()
    kwin[0] = kt[:, pl.ds(0, tok)].T
    loads[1].wait()
    for n in range(LAT_C // LANES):
        at = pl.ds(n * LANES, LANES)
        gf[n] = graw[:, at].astype(jnp.float32)
        for h in range(heads):
            g[pl.ds(h * tok, tok), at] = gf[n, pl.ds(h, tok, stride=heads), :].astype(jnp.bfloat16)
    for load in loads[2:]:
        load.wait()
    scores(0, 1)

    pl.semaphore_wait(barrier, len(peers))

    for k in STRAIGHT:
        go(g_z(k, k))

    def spread(n):
        for j in range(1, nx):
            go(g_x(n, j))

    def across(n):
        for j in range(1, nx):
            g_x(n, j).wait_recv()
        go(g_c(n))

    def take(n):
        g_c(n).wait_recv()
        k, count = GROUPS[n]
        scores(k, count)
        for extra in range(count):
            turn(k + extra)

    def relay(k):
        g_z(k, k).wait_recv()
        for later in RELAYED[k]:
            go(g_z(later, later - k))

    relay(3)
    g_z(1, 1).wait_recv()
    g_z(2, 2).wait_recv()
    spread(0)
    spread(1)
    relay(6)
    spread(2)
    across(0)
    across(1)
    g_z(4, 1).wait_recv()
    g_z(5, 2).wait_recv()
    spread(3)
    across(2)
    take(0)
    g_z(7, 1).wait_recv()
    g_z(8, 2).wait_recv()
    spread(4)
    take(1)
    across(3)
    take(2)
    across(4)
    take(3)
    take(4)

    def soften(n, _):
        width = SOFT_HEADS * tok
        at = pl.ds(pl.multiple_of(n * width, width), width)
        over = 1.0 / tops[span + 1 : span + 2, at]
        final = tops[span + 2 : span + 3, at]
        delta = jnp.zeros((1, width), jnp.float32)
        for k in range(span + 1):
            here = pl.ds(k * tok, tok)
            weight = ew[here, at] * (jnp.exp2((tops[k : k + 1, at] - final) * exp2_scale) * over)
            prob = weight.astype(jnp.bfloat16)
            pw[here, at] = prob
            ew[here, at] = weight
            delta = delta + jnp.sum(prob.astype(jnp.float32) * gp[here, at], axis=0, keepdims=True)
        for k in range(span + 1):
            here = pl.ds(k * tok, tok)
            ds[here, at] = (ew[here, at] * (gp[here, at] - delta) * score_scale).astype(jnp.bfloat16)
        return 0

    lax.fori_loop(0, heads // SOFT_HEADS, soften, 0)

    def r_c(n):
        at = pl.ds(*BACK[n])
        return remote(csend.at[at], crecv.at[at], rc_s.at[n], rc_r.at[n], (s, x * 2 + 1 - c))

    def r_x(n, j):
        src = xsend.at[pl.ds(*BACK[n]), pl.ds(pl.multiple_of(xpeer(j) * piece, 16), piece)]
        dst = xrecv.at[j - 1, pl.ds(*BACK[n])]
        at = n * (nx - 1) + j - 1
        return remote(src, dst, rx_s.at[at], rx_r.at[at], (s, xpeer(j) * 2 + c))

    def r_z(k, step):
        return remote(zsend.at[k - 1], zrecv.at[k - 1], rz_s.at[k - 1], rz_r.at[k - 1], (ctx(-step), hd))

    def products(n):
        k, count = BACK[n]
        here = pl.ds(k * tok, count * tok)
        low, high = pl.multiple_of(c * half, 16), pl.multiple_of((1 - c) * half, 16)
        part[here, :] = lax.dot_general(ds[here, :], q[...], NT, preferred_element_type=jnp.float32)
        part[here, :LAT_C] += jnp.dot(pw[here, :], g[...], preferred_element_type=jnp.float32)
        for e in range(k, k + count):
            csend[e] = part[pl.ds(pl.multiple_of(e * tok + high, 16), half), :].astype(jnp.bfloat16)
        go(r_c(n))

    def pair(n):
        r_c(n).wait_recv()
        k, count = BACK[n]
        for e in range(k, k + count):
            at = pl.ds(pl.multiple_of(e * tok + c * half, 16), half)
            total = part[at, :] + crecv[e].astype(jnp.float32)
            part[at, :] = total
            xsend[e] = total.astype(jnp.bfloat16)
        for j in range(1, nx):
            go(r_x(n, j))

    def chips(n):
        for j in range(1, nx):
            r_x(n, j).wait_recv()

    def mine_of(k):
        total = part[pl.ds(pl.multiple_of(k * tok + mine, 16), piece), :]
        for j in range(1, nx):
            total = total + xrecv[j - 1, k].astype(jnp.float32)
        return total

    def leaf(k, step):
        zsend[k - 1] = mine_of(k).astype(jnp.bfloat16)
        go(r_z(k, step))

    def node(k):
        total = mine_of(k)
        for later in RELAYED[k]:
            r_z(later, later - k).wait_recv()
            total = total + zrecv[later - 1].astype(jnp.float32)
        zsend[k - 1] = total.astype(jnp.bfloat16)
        go(r_z(k, k))

    outs = []

    def queries(n):
        width = Q_HEADS * tok
        at = pl.ds(n * width, width)
        gqbuf[:, at] = jnp.dot(kt[...], ds[:, at], preferred_element_type=jnp.float32).astype(jnp.bfloat16)
        for h in range(n * Q_HEADS, (n + 1) * Q_HEADS):
            out = pltpu.make_async_copy(gqbuf.at[:, pl.ds(h * tok, tok)], gq_hbm.at[h], local.at[2 + h])
            out.start()
            outs.append(out)

    def ag(j):
        ref = glbuf.at[pl.ds(mine, piece)]
        return remote(ref, ref, ag_s.at[j - 1], ag_r.at[j - 1], (s, lax.rem(hd + j, nhead)))

    products(0)
    products(1)
    pair(0)
    products(2)
    pair(1)
    products(3)
    pair(2)
    products(4)
    pair(3)
    products(5)
    chips(0)
    leaf(8, 2)
    leaf(7, 1)
    pair(4)
    chips(1)
    leaf(5, 2)
    leaf(4, 1)
    pair(5)
    queries(0)
    chips(2)
    node(6)
    chips(3)
    node(3)
    chips(4)
    leaf(2, 2)
    leaf(1, 1)
    queries(1)
    queries(2)
    queries(3)
    chips(5)
    total = mine_of(0)
    for k in reversed(STRAIGHT):
        r_z(k, k).wait_recv()
        total = total + zrecv[k - 1].astype(jnp.float32)
    glbuf[pl.ds(mine, piece), :] = total.astype(jnp.bfloat16)
    for j in range(1, nhead):
        go(ag(j))
    for out in outs:
        out.wait()
    for j in range(1, nhead):
        ag(j).wait_recv()
    last = pltpu.make_async_copy(glbuf, gl_hbm, local.at[0])
    last.start()
    for copy in sent:
        copy.wait_send()
    last.wait()


def on_device(nctx, nhead, span, queries, latents, grad_out, doc_ids):
    tok, heads, lat = queries.shape
    rows = tok * heads
    window = (span + 1) * tok
    piece, nx = tok // nhead, nhead // 2
    bf16, f32 = jnp.bfloat16, jnp.float32
    dma = pltpu.SemaphoreType.DMA
    groups, back = len(GROUPS), len(BACK)
    grad_queries, grad_latents = pl.pallas_call(
        functools.partial(kernel, span, nctx, nhead),
        out_shape=(
            jax.ShapeDtypeStruct((heads, lat, tok), bf16),
            jax.ShapeDtypeStruct((tok, lat), bf16),
        ),
        in_specs=[pl.BlockSpec(memory_space=pltpu.VMEM)] + [pl.BlockSpec(memory_space=pltpu.HBM)] * 3,
        out_specs=(pl.BlockSpec(memory_space=pltpu.HBM), pl.BlockSpec(memory_space=pl.ANY)),
        scratch_shapes=[
            pltpu.VMEM((span + 1, tok, lat), bf16),
            pltpu.VMEM((lat, window), bf16),
            pltpu.VMEM((lat, rows), bf16),
            pltpu.VMEM((rows, LAT_C), bf16),
            pltpu.VMEM((LAT_C // LANES, rows, LANES), f32),
            pltpu.VMEM((rows, LAT_C), bf16),
            pltpu.VMEM((window, rows), f32),
            pltpu.VMEM((window, rows), f32),
            pltpu.VMEM((window, rows), bf16),
            pltpu.VMEM((window, rows), bf16),
            pltpu.VMEM((span + 3, rows), f32),
            pltpu.VMEM((window, lat), f32),
            pltpu.VMEM((span + 1, tok // 2, lat), bf16),
            pltpu.VMEM((span + 1, tok // 2, lat), bf16),
            pltpu.VMEM((span + 1, tok // 2, lat), bf16),
            pltpu.VMEM((nx - 1, span + 1, piece, lat), bf16),
            pltpu.VMEM((span, piece, lat), bf16),
            pltpu.VMEM((span, piece, lat), bf16),
            pltpu.VMEM((lat, rows), bf16),
            pltpu.VMEM((tok, lat), bf16),
            dma((2 + heads,)),
            dma((span,)), dma((span,)),
            dma((groups * (nx - 1),)), dma((groups * (nx - 1),)),
            dma((groups,)), dma((groups,)),
            dma((back,)), dma((back,)),
            dma((back * (nx - 1),)), dma((back * (nx - 1),)),
            dma((span,)), dma((span,)),
            dma((nhead - 1,)), dma((nhead - 1,)),
        ],
        compiler_params=pltpu.CompilerParams(
            collective_id=0, has_side_effects=True, vmem_limit_bytes=56 * 1024 * 1024
        ),
    )(doc_ids.reshape(nctx, tok), queries.transpose(1, 2, 0), grad_out.reshape(rows, LAT_C), latents.T)
    return grad_queries.transpose(2, 0, 1), grad_latents


def solution(mesh):
    nctx, nhead = mesh.shape["ctx"], mesh.shape["head"]
    placed = (P("ctx", "head", None), P("ctx", None), P("ctx", "head", None), P())
    return jax.shard_map(
        functools.partial(on_device, nctx, nhead, SPAN),
        mesh=mesh,
        in_specs=placed,
        out_specs=(P("ctx", "head", None), P("ctx", None)),
        check_vma=False,
    )
```

time: 378 us -> 69.7 us (0.18)
  the two profiles are of different devices: /device:TPU:16 before, /device:TPU:1 now
where the time goes in v2:
time: 69.7 us; the launch traced here: 69.4 us
  Pallas kernels  64.7 us (93%)
  local copies, waits for them, and re-layouts  4.06 us (6%)
    pallas_call x1, Pallas kernels, on_device(): pl.pallas_call(functools.partial(kernel, span, nctx, nhead), out_shape=(j...  64.7 us
    unnamed x2, local copies, waits for them, and re-layouts  4.06 us

profile of v2, /device:TPU:1, one launch (start us, length us, event | category | flops | bytes accessed | tf_op | source)
XLA Modules:
  0.0 69.4 jit_solution(5046596327487884511)
XLA Ops:
  0.6 64.7 %shard_map.59 = (bf16[8,576,128]{2,1,0:T(8,128)(2,1)}, bf16[128,576]{1,0:T(8,128)(2,1)}) custom-call(s32[64,128]{1,0:T(8,128)} %bitcast.9, bf16[8,576,128]{2,1,0:T(8,128)(2,1)} %bitcast.5, bf16[1024,512]{1,0:T(8,128)(2,1)} %bitcast.7, bf16[576,128]{1,0:T(8,128)(2,1)} %bitcast.8), custom_call_target="tpu_custom_call" | custom-call | tf_op jit(solution)/shard_map/pallas_call | solution.py:338
  65.3 1.7 %copy.6 = bf16[128,576]{0,1:T(8,128)(2,1)} copy(bf16[128,576]{1,0:T(8,128)(2,1)} %get-tuple-element.7) | data formatting | bytes 294912
  67.0 2.4 %copy.8 = bf16[128,8,576]{0,2,1:T(8,128)(2,1)} copy(bf16[128,8,576]{0,2,1:T(8,128)(2,1)} %bitcast.6) | data formatting | bytes 2359296

commit v3 on v2

--- a/solution.py
+++ b/solution.py
@@ -21,15 +21,29 @@
 NT = (((1,), (1,)), ((), ()))
 
 STRAIGHT = (6, 3, 2, 1)
+FROM = {1: 1, 2: 2, 3: 3, 6: 6, 4: 1, 5: 2, 7: 1, 8: 2}
+FIRST = (6, 3, 2, 1)
+DIRECT = ()
+GATHER = (
+    ("arrive", 3), ("arrive", 1), ("arrive", 2), ("spread", 0), ("spread", 1), ("arrive", 6), ("spread", 2), ("across", 0),
+    ("across", 1), ("arrive", 4), ("arrive", 5), ("spread", 3), ("across", 2), ("take", 0), ("arrive", 7), ("arrive", 8),
+    ("spread", 4), ("take", 1), ("across", 3), ("take", 2), ("across", 4), ("take", 3), ("take", 4),
+)
 RELAYED = {3: (5, 4), 6: (8, 7)}
 GROUPS = ((1, 2), (3, 1), (6, 1), (4, 2), (7, 2))
 BACK = ((7, 2), (4, 2), (6, 1), (3, 1), (1, 2), (0, 1))
+RETURN = (
+    ("products", 0), ("products", 1), ("pair", 0), ("products", 2), ("pair", 1), ("products", 3), ("pair", 2),
+    ("products", 4), ("chips", 0), ("leaves", 7), ("pair", 3), ("products", 5), ("pair", 4), ("chips", 1), ("leaves", 4),
+    ("pair", 5), ("chips", 2), ("node", 6), ("chips", 3), ("node", 3), ("chips", 4), ("leaves", 1),
+    ("queries", 0), ("queries", 1), ("queries", 2), ("queries", 3), ("chips", 5),
+)
 
 
 def kernel(
     span, nctx, nhead,
     doc_ref, q_hbm, g_hbm, lat_hbm, gq_hbm, gl_hbm,
-    kwin, kt, q, graw, gf, g, ew, gp, pw, ds, tops, part, csend, crecv, xsend, xrecv, zsend, zrecv, gqbuf, glbuf,
+    kwin, kt, q, graw, gf, g, ew, gp, pw, ds, tops, part, csend, crecv, xsend, xrecv, zsend, zrecv, gqbuf, glbuf, glturn,
     local, gz_s, gz_r, gx_s, gx_r, gc_s, gc_r, rc_s, rc_r, rx_s, rx_r, rz_s, rz_r, ag_s, ag_r,
 ):
     heads, lat, tok = q_hbm.shape
@@ -76,8 +90,9 @@
 
     def g_x(n, j):
         ref = kwin.at[pl.ds(*GROUPS[n]), pl.ds(mine, piece)]
-        at = n * (nx - 1) + j - 1
-        return remote(ref, ref, gx_s.at[at], gx_r.at[at], (s, xpeer(j) * 2 + c))
+        at = n * (nhead - 1) + j - 1
+        peer = lax.rem(hd + j, nhead) if n in DIRECT else xpeer(j) * 2 + c
+        return remote(ref, ref, gx_s.at[at], gx_r.at[at], (s, peer))
 
     def g_c(n):
         ref = kwin.at[pl.ds(*GROUPS[n]), pl.ds(pl.multiple_of(c * half, 16), half)]
@@ -128,6 +143,10 @@
 
     loads[0].wait()
     kwin[0] = kt[:, pl.ds(0, tok)].T
+    pl.semaphore_wait(barrier, len(peers))
+    for k in FIRST:
+        go(g_z(k, k))
+
     loads[1].wait()
     for n in range(LAT_C // LANES):
         at = pl.ds(n * LANES, LANES)
@@ -138,55 +157,36 @@
         load.wait()
     scores(0, 1)
 
-    pl.semaphore_wait(barrier, len(peers))
-
-    for k in STRAIGHT:
-        go(g_z(k, k))
-
     def spread(n):
-        for j in range(1, nx):
+        for j in range(1, nhead if n in DIRECT else nx):
             go(g_x(n, j))
 
     def across(n):
-        for j in range(1, nx):
+        for j in range(1, nhead if n in DIRECT else nx):
             g_x(n, j).wait_recv()
-        go(g_c(n))
+        if n not in DIRECT:
+            go(g_c(n))
 
     def take(n):
-        g_c(n).wait_recv()
+        if n not in DIRECT:
+            g_c(n).wait_recv()
         k, count = GROUPS[n]
         scores(k, count)
         for extra in range(count):
             turn(k + extra)
 
-    def relay(k):
-        g_z(k, k).wait_recv()
-        for later in RELAYED[k]:
+    def arrive(k):
+        step = FROM[k]
+        g_z(k, step).wait_recv()
+        for later in RELAYED.get(k, ()):
             go(g_z(later, later - k))
 
-    relay(3)
-    g_z(1, 1).wait_recv()
-    g_z(2, 2).wait_recv()
-    spread(0)
-    spread(1)
-    relay(6)
-    spread(2)
-    across(0)
-    across(1)
-    g_z(4, 1).wait_recv()
-    g_z(5, 2).wait_recv()
-    spread(3)
-    across(2)
-    take(0)
-    g_z(7, 1).wait_recv()
-    g_z(8, 2).wait_recv()
-    spread(4)
-    take(1)
-    across(3)
-    take(2)
-    across(4)
-    take(3)
-    take(4)
+    def send(k):
+        go(g_z(k, k))
+
+    steps = {"send": send, "arrive": arrive, "spread": spread, "across": across, "take": take}
+    for op, n in GATHER:
+        steps[op](n)
 
     def soften(n, _):
         width = SOFT_HEADS * tok
@@ -279,36 +279,14 @@
         ref = glbuf.at[pl.ds(mine, piece)]
         return remote(ref, ref, ag_s.at[j - 1], ag_r.at[j - 1], (s, lax.rem(hd + j, nhead)))
 
-    products(0)
-    products(1)
-    pair(0)
-    products(2)
-    pair(1)
-    products(3)
-    pair(2)
-    products(4)
-    pair(3)
-    products(5)
-    chips(0)
-    leaf(8, 2)
-    leaf(7, 1)
-    pair(4)
-    chips(1)
-    leaf(5, 2)
-    leaf(4, 1)
-    pair(5)
-    queries(0)
-    chips(2)
-    node(6)
-    chips(3)
-    node(3)
-    chips(4)
-    leaf(2, 2)
-    leaf(1, 1)
-    queries(1)
-    queries(2)
-    queries(3)
-    chips(5)
+    def leaves(k):
+        leaf(k + 1, 2)
+        leaf(k, 1)
+
+    steps = {"products": products, "pair": pair, "chips": chips, "leaves": leaves, "node": node, "queries": queries}
+    for op, n in RETURN:
+        steps[op](n)
+
     total = mine_of(0)
     for k in reversed(STRAIGHT):
         r_z(k, k).wait_recv()
@@ -320,7 +298,8 @@
         out.wait()
     for j in range(1, nhead):
         ag(j).wait_recv()
-    last = pltpu.make_async_copy(glbuf, gl_hbm, local.at[0])
+    glturn[...] = glbuf[...].T
+    last = pltpu.make_async_copy(glturn, gl_hbm, local.at[0])
     last.start()
     for copy in sent:
         copy.wait_send()
@@ -339,7 +318,7 @@
         functools.partial(kernel, span, nctx, nhead),
         out_shape=(
             jax.ShapeDtypeStruct((heads, lat, tok), bf16),
-            jax.ShapeDtypeStruct((tok, lat), bf16),
+            jax.ShapeDtypeStruct((lat, tok), bf16),
         ),
         in_specs=[pl.BlockSpec(memory_space=pltpu.VMEM)] + [pl.BlockSpec(memory_space=pltpu.HBM)] * 3,
         out_specs=(pl.BlockSpec(memory_space=pltpu.HBM), pl.BlockSpec(memory_space=pl.ANY)),
@@ -364,9 +343,10 @@
             pltpu.VMEM((span, piece, lat), bf16),
             pltpu.VMEM((lat, rows), bf16),
             pltpu.VMEM((tok, lat), bf16),
+            pltpu.VMEM((lat, tok), bf16),
             dma((2 + heads,)),
             dma((span,)), dma((span,)),
-            dma((groups * (nx - 1),)), dma((groups * (nx - 1),)),
+            dma((groups * (nhead - 1),)), dma((groups * (nhead - 1),)),
             dma((groups,)), dma((groups,)),
             dma((back,)), dma((back,)),
             dma((back * (nx - 1),)), dma((back * (nx - 1),)),
@@ -377,7 +357,7 @@
             collective_id=0, has_side_effects=True, vmem_limit_bytes=56 * 1024 * 1024
         ),
     )(doc_ids.reshape(nctx, tok), queries.transpose(1, 2, 0), grad_out.reshape(rows, LAT_C), latents.T)
-    return grad_queries.transpose(2, 0, 1), grad_latents
+    return grad_queries.transpose(2, 0, 1), grad_latents.T
 
 
 def solution(mesh):

time: 69.7 us -> 69.2 us (level)
  local copies, waits for them, and re-layouts: 4.06 us -> 3.07 us
    unnamed x2 -> x4, local copies, waits for them, and re-layouts: 4.06 us -> 3.07 us
where the time goes in v3:
time: 69.2 us; the launch traced here: 68.9 us
  Pallas kernels  65.2 us (94%)
  local copies, waits for them, and re-layouts  3.07 us (4%)
    pallas_call x1, Pallas kernels, on_device(): pl.pallas_call(functools.partial(kernel, span, nctx, nhead), out_shape=(j...  65.2 us
    unnamed x4, local copies, waits for them, and re-layouts  3.07 us

profile of v3, /device:TPU:1, one launch (start us, length us, event | category | flops | bytes accessed | tf_op | source)
XLA Modules:
  0.0 68.9 jit_solution(3124968437537382032)
XLA Ops:
  0.6 65.2 %shard_map.59 = (bf16[8,576,128]{2,1,0:T(8,128)(2,1)}, bf16[576,128]{1,0:T(8,128)(2,1)}) custom-call(s32[64,128]{1,0:T(8,128)} %bitcast.11, bf16[8,576,128]{2,1,0:T(8,128)(2,1)} %bitcast.6, bf16[1024,512]{1,0:T(8,128)(2,1)} %bitcast.8, bf16[576,128]{1,0:T(8,128)(2,1)} %bitcast.9), custom_call_target="tpu_custom_call" | custom-call | tf_op jit(solution)/shard_map/pallas_call | solution.py:317
  65.9 0.0 copy-start
  65.9 2.4 %copy.8 = bf16[128,8,576]{0,2,1:T(8,128)(2,1)} copy(bf16[128,8,576]{0,2,1:T(8,128)(2,1)} %bitcast.7) | data formatting | bytes 2359296
  68.3 0.0 copy-done
  68.3 0.7 copy.9
Async XLA Ops:
  65.9 2.4 %copy-start = (bf16[576,128]{1,0:T(8,128)(2,1)S(1)}, bf16[576,128]{1,0:T(8,128)(2,1)}, u32[]{:S(2)}) copy-start(bf16[576,128]{1,0:T(8,128)(2,1)} %get-tuple-element.5) | copy-start | bytes 442372

commit v4 on v3

--- a/solution.py
+++ b/solution.py
@@ -10,7 +10,7 @@
 LAT_C = 512
 SPAN = 8
 LANES = 128
-SC_HEADS = 4
+SC_HEADS = 8
 SOFT_HEADS = 2
 Q_HEADS = 2
 

time: 69.2 us -> 68.5 us (0.990)
  Pallas kernels: 65.2 us -> 64.5 us
where the time goes in v4:
time: 68.5 us; the launch traced here: 68.3 us
  Pallas kernels  64.5 us (94%)
  local copies, waits for them, and re-layouts  3.07 us (4%)
    pallas_call x1, Pallas kernels, on_device(): pl.pallas_call(functools.partial(kernel, span, nctx, nhead), out_shape=(j...  64.5 us
    unnamed x4, local copies, waits for them, and re-layouts  3.07 us

profile of v4, /device:TPU:1, one launch (start us, length us, event | category | flops | bytes accessed | tf_op | source)
XLA Modules:
  0.0 68.3 jit_solution(9279922688954146979)
XLA Ops:
  0.6 64.5 %shard_map.59 = (bf16[8,576,128]{2,1,0:T(8,128)(2,1)}, bf16[576,128]{1,0:T(8,128)(2,1)}) custom-call(s32[64,128]{1,0:T(8,128)} %bitcast.11, bf16[8,576,128]{2,1,0:T(8,128)(2,1)} %bitcast.6, bf16[1024,512]{1,0:T(8,128)(2,1)} %bitcast.8, bf16[576,128]{1,0:T(8,128)(2,1)} %bitcast.9), custom_call_target="tpu_custom_call" | custom-call | tf_op jit(solution)/shard_map/pallas_call | solution.py:317
  65.2 0.0 copy-start
  65.2 2.4 %copy.8 = bf16[128,8,576]{0,2,1:T(8,128)(2,1)} copy(bf16[128,8,576]{0,2,1:T(8,128)(2,1)} %bitcast.7) | data formatting | bytes 2359296
  67.6 0.0 copy-done
  67.6 0.7 copy.9
Async XLA Ops:
  65.2 2.4 %copy-start = (bf16[576,128]{1,0:T(8,128)(2,1)S(1)}, bf16[576,128]{1,0:T(8,128)(2,1)}, u32[]{:S(2)}) copy-start(bf16[576,128]{1,0:T(8,128)(2,1)} %get-tuple-element.5) | copy-start | bytes 442372
